TPU v7x, 32 devices: a whole 2x2x4 slice. The times are simulated.
32 devices in a mesh: groups: 2 (over x), orb: 16 (over z, y, core).
Axes of the slice: x: 2, y: 2, z: 4, core: 2. Of those that a mesh axis runs over, the one named last changes fastest.
Arguments:
- blocks: bfloat16 [192, 1536, 384], P(('groups', 'orb')), parts along dimension 0, may hold values from -1 to 1
- pao_energy: float32 [192, 384], P(('groups', 'orb')), parts along dimension 0, may hold values from 0.5 to 3
- occ_energy: float32 [192], P(('groups', 'orb')), parts along dimension 0, may hold values from -1.5 to -0.3
- dom_blocks: int32 [192], P(('groups', 'orb')), parts along dimension 0, may hold values from 1 to 3
- pairs: int32 [512, 2], P(('groups', 'orb')), parts along dimension 0, may hold values from -1 to 95, as said below
Outputs:
- pair_energy: float32 [512], P(('groups', 'orb')), parts along dimension 0
- density: float32 [192, 384, 384], P(('groups', 'orb')), parts along dimension 0
There are 2 independent parts, one for each index of `groups`. A program takes and returns all parts, laid end to end along the dimension named above; each array names one. Nothing has to cross between parts.
Inputs may be any that keep to these rules, and one draw needn't show every extreme that they name: `pairs`: the slots of device d are rows d * 16 to (d + 1) * 16 - 1; the live ones come first, their first orbital is owned by d (one of orbitals d * 6 to (d + 1) * 6 - 1) and their second orbital is a different orbital owned by d - 1, d or d + 1. A device has 1 to 16 live slots; in every draw some device has all 16 live and some device only one. Empty slots hold -1 twice.
All inputs are finite; a program needn't handle non-finite values.
Results may differ from a plain program's by a relative error of at most 0.0021.
Values may be sent and summed in bfloat16 or wider, within the bound.
A program may use at most 128 MiB of HBM per device.

v0:
```python
import math

import jax
import jax.numpy as jnp
from jax import lax
from jax.sharding import PartitionSpec as P

GRAIN = 128


def extended(x, sides, width):
    for axis, dim in sides:
        size, length = (lax.axis_size(axis), x.shape[dim])
        up = [(i, (i + 1) % size) for i in range(size - 1)]
        down = [(j, i) for i, j in up]
        last = lax.slice_in_dim(x, length - width, length, axis=dim)
        leading = lax.slice_in_dim(x, 0, width, axis=dim)
        before = lax.ppermute(last, axis, up)
        after = lax.ppermute(leading, axis, down)
        x = jnp.concatenate([before, x, after], axis=dim)
    return x


def from_behind(block, axis, distance):
    devices = range(lax.axis_size(axis))
    route = [(i - distance, i) for i in devices if i - distance in devices]
    return lax.ppermute(block, axis, route)


def take_row(stack, where):
    return lax.dynamic_index_in_dim(stack, where, 0, keepdims=False)


def add_row(stack, where, term):
    return lax.dynamic_update_index_in_dim(stack, take_row(stack, where) + term, where, 0)


def per_device(blocks, pao_energy, occ_energy, dom_blocks, pairs):
    orb_dev = blocks.shape[0]
    width = blocks.shape[2]
    factor = 1.0 / math.sqrt(width)
    column = lax.broadcasted_iota(jnp.int32, (orb_dev, width), 1)
    live_cols = column < (dom_blocks * GRAIN)[:, None]
    masked = jnp.where(live_cols[:, None, :], blocks, jnp.zeros((), blocks.dtype))
    shifted = pao_energy - occ_energy[:, None]
    window_blocks = extended(masked, (("orb", 0),), orb_dev)
    window_energy = extended(shifted, (("orb", 0),), orb_dev)
    my_start = lax.axis_index("orb") * orb_dev
    base = my_start - orb_dev
    square = jnp.zeros((width, width), jnp.float32)

    def pair_work(pair):
        left_at = jnp.clip(pair[0] - base, 0, 3 * orb_dev - 1)
        right_at = jnp.clip(pair[1] - base, 0, 3 * orb_dev - 1)
        left_block = take_row(window_blocks, left_at)
        right_block = take_row(window_blocks, right_at)
        exchange = lax.dot_general(
            left_block, right_block, (((0,), (0,)), ((), ())), preferred_element_type=jnp.float32
        )
        denom = (
            take_row(window_energy, left_at)[:, None] + take_row(window_energy, right_at)[None, :]
        )
        amplitude = -exchange / denom
        energy = 2.0 * jnp.sum(exchange * amplitude)
        rounded = amplitude.astype(jnp.bfloat16)
        first_part = jnp.dot(rounded, rounded.T, preferred_element_type=jnp.float32) * factor
        second_part = (
            lax.dot_general(
                rounded, rounded, (((0,), (0,)), ((), ())), preferred_element_type=jnp.float32
            )
            * factor
        )
        return (energy, rounded, first_part, second_part)

    def pair_skip(pair):
        return (jnp.zeros((), jnp.float32), jnp.zeros((width, width), jnp.bfloat16), square, square)

    def pair_step(carry, pair):
        own, window_acc = carry
        live = pair[0] >= 0
        energy, rounded, first_part, second_part = lax.cond(live, pair_work, pair_skip, pair)
        own_at = jnp.clip(pair[0] - my_start, 0, orb_dev - 1)
        own = add_row(own, own_at, first_part)
        right_at = jnp.clip(pair[1] - base, 0, 3 * orb_dev - 1)
        window_acc = add_row(window_acc, right_at, second_part)
        return ((own, window_acc), (energy, rounded))

    own = jnp.zeros((orb_dev, width, width), jnp.float32)
    window_acc = jnp.zeros((3 * orb_dev, width, width), jnp.float32)
    (own, window_acc), (energies, amplitudes) = lax.scan(pair_step, (own, window_acc), pairs)
    from_right = from_behind(window_acc[:orb_dev], "orb", -1)
    from_left = from_behind(window_acc[2 * orb_dev :], "orb", 1)
    density = own + window_acc[orb_dev : 2 * orb_dev] + from_right + from_left
    return (energies, density)


def solution(mesh):
    in_specs = (
        P(("groups", "orb"), None, None),
        P(("groups", "orb"), None),
        P(("groups", "orb")),
        P(("groups", "orb")),
        P(("groups", "orb"), None),
    )
    out_specs = (P(("groups", "orb")), P(("groups", "orb"), None, None))
    return jax.shard_map(
        per_device, mesh=mesh, in_specs=in_specs, out_specs=out_specs, check_vma=False
    )
```

profile of v0, /device:TPU:9, one launch (start us, length us, event | category | flops | bytes accessed | tf_op | source)
XLA Modules:
  0.0 484.9 jit_solution(4166035463982370519)
XLA Ops:
  1.4 6.7 %broadcast_select_fusion = bf16[6,1536,384]{2,1,0:T(8,128)(2,1)} fusion(bf16[6,1536,384]{2,1,0:T(8,128)(2,1)} %param.9, pred[6,384]{1,0:T(8,128)(4,1)S(1)} %iota_compare_fusion), kind=kLoop, calls=%fused_computation.21 | loop fusion | flops 3538944 | bytes 14158080 | tf_op jit(solution)/shard_map/jit(_where)/select_n | solution.py:44
  8.0 2.6 collective-permute-start.1
  10.6 3.0 collective-permute-start
  15.7 3.6 collective-permute-start.2
  19.4 145.7 %collective-permute-done.3 = f32[6,384]{1,0:T(8,128)S(1)} collective-permute-done((f32[6,384]{1,0:T(8,128)S(1)}, f32[6,384]{1,0:T(8,128)S(1)}, u32[]{:S(2)}, u32[]{:S(2)}) %collective-permute-start.3) | collective-permute-done | bytes 9248 | tf_op jit(solution)/shard_map/ppermute | solution.py:19
  165.3 19.6 %pad_maximum_fusion = bf16[18,1536,384]{2,1,0:T(8,128)(2,1)} fusion(bf16[6,1536,384]{2,1,0:T(8,128)(2,1)} %collective-permute-done.1, bf16[6,1536,384]{2,1,0:T(8,128)(2,1)} %broadcast_select_fusion, bf16[6,1536,384]{2,1,0:T(8,128)(2,1)} %collective-permute-done), kind=kLoop, calls=%fused_computation.20 | loop fusion | flops 21233664 | bytes 42467328 | tf_op jit(solution)/shard_map/concatenate | solution.py:20
  186.9 5.1 %broadcast_in_dim.39 = f32[18,384,384]{2,1,0:T(8,128)} broadcast(f32[]{:T(128)} %constant.69.clone.1), dimensions={} | broadcast | bytes 10616836 | tf_op jit(solution)/shard_map/broadcast_in_dim | solution.py:89
  192.0 140.2 %while.14 = (s32[]{:T(128)}, f32[6,384,384]{2,1,0:T(8,128)}, f32[18,384,384]{2,1,0:T(8,128)}, f32[16]{0:T(128)S(1)}, s32[16,2]{1,0:T(8,128)S(1)}, /*index=5*/s32...) while((s32[]{:T(128)}, f32[6,384,384]{2,1,0:T(8,128)}, ...), condition=%wide.region_4.5_spmd, body=%wide.region_0.4_spmd.sunk | while | flops 681984000 | bytes 11222475 | solution.py:90
  196.9 6.9 %conditional.2 = (f32[]{:T(128)}, f32[384,384]{1,0:T(8,128)S(1)}, f32[384,384]{1,0:T(8,128)S(1)}) conditional(s32[]{:T(128)} %convert_element_type.10, () %tuple.43, (s32[1,2]{1,0:T(1,128)S(1)}, s32[]{:T(128)}, bf16[18,1536,384]{2,1,0:T(8,128)(2,1)}, f32[18,384]{1,0:T(8,128)S(1)}) %tuple.44), branch_computations={%region_1.1_spmd, %region_2.3_spmd} | conditional | flops 681689088 | bytes 5323920 | solution.py:81
  198.9 3.2 multiply_reduce_fusion
  209.9 6.9 %conditional.2 = (f32[]{:T(128)}, f32[384,384]{1,0:T(8,128)S(1)}, f32[384,384]{1,0:T(8,128)S(1)}) conditional(s32[]{:T(128)} %convert_element_type.10, () %tuple.43, (s32[1,2]{1,0:T(1,128)S(1)}, s32[]{:T(128)}, bf16[18,1536,384]{2,1,0:T(8,128)(2,1)}, f32[18,384]{1,0:T(8,128)S(1)}) %tuple.44), branch_computations={%region_1.1_spmd, %region_2.3_spmd} | conditional | flops 681689088 | bytes 5323920 | solution.py:81
  211.9 3.1 multiply_reduce_fusion
  222.9 6.9 %conditional.2 = (f32[]{:T(128)}, f32[384,384]{1,0:T(8,128)S(1)}, f32[384,384]{1,0:T(8,128)S(1)}) conditional(s32[]{:T(128)} %convert_element_type.10, () %tuple.43, (s32[1,2]{1,0:T(1,128)S(1)}, s32[]{:T(128)}, bf16[18,1536,384]{2,1,0:T(8,128)(2,1)}, f32[18,384]{1,0:T(8,128)S(1)}) %tuple.44), branch_computations={%region_1.1_spmd, %region_2.3_spmd} | conditional | flops 681689088 | bytes 5323920 | solution.py:81
  225.0 3.1 multiply_reduce_fusion
  235.9 6.9 %conditional.2 = (f32[]{:T(128)}, f32[384,384]{1,0:T(8,128)S(1)}, f32[384,384]{1,0:T(8,128)S(1)}) conditional(s32[]{:T(128)} %convert_element_type.10, () %tuple.43, (s32[1,2]{1,0:T(1,128)S(1)}, s32[]{:T(128)}, bf16[18,1536,384]{2,1,0:T(8,128)(2,1)}, f32[18,384]{1,0:T(8,128)S(1)}) %tuple.44), branch_computations={%region_1.1_spmd, %region_2.3_spmd} | conditional | flops 681689088 | bytes 5323920 | solution.py:81
  238.0 3.1 multiply_reduce_fusion
  249.0 6.9 %conditional.2 = (f32[]{:T(128)}, f32[384,384]{1,0:T(8,128)S(1)}, f32[384,384]{1,0:T(8,128)S(1)}) conditional(s32[]{:T(128)} %convert_element_type.10, () %tuple.43, (s32[1,2]{1,0:T(1,128)S(1)}, s32[]{:T(128)}, bf16[18,1536,384]{2,1,0:T(8,128)(2,1)}, f32[18,384]{1,0:T(8,128)S(1)}) %tuple.44), branch_computations={%region_1.1_spmd, %region_2.3_spmd} | conditional | flops 681689088 | bytes 5323920 | solution.py:81
  251.0 3.1 multiply_reduce_fusion
  262.0 6.9 %conditional.2 = (f32[]{:T(128)}, f32[384,384]{1,0:T(8,128)S(1)}, f32[384,384]{1,0:T(8,128)S(1)}) conditional(s32[]{:T(128)} %convert_element_type.10, () %tuple.43, (s32[1,2]{1,0:T(1,128)S(1)}, s32[]{:T(128)}, bf16[18,1536,384]{2,1,0:T(8,128)(2,1)}, f32[18,384]{1,0:T(8,128)S(1)}) %tuple.44), branch_computations={%region_1.1_spmd, %region_2.3_spmd} | conditional | flops 681689088 | bytes 5323920 | solution.py:81
  264.0 3.1 multiply_reduce_fusion
  332.2 3.7 fusion.11
  337.8 72.5 %collective-permute-start.5 = (f32[6,384,384]{2,1,0:T(8,128)S(1)}, f32[6,384,384]{2,1,0:T(8,128)S(1)}, u32[]{:S(2)}, u32[]{:S(2)}) collective-permute-start(f32[6,384,384]{2,1,0:T(8,128)S(1)} %get-tuple-element.108), channel_id=1, source_target_pairs={{0,1},{1,2},{2,3},{3,4},{4,5},{5,6},{6,7},{7,8},{8,9},{9,10},{10,1... | collective-permute-start | bytes 10616840 | tf_op jit(solution)/shard_map/ppermute | solution.py:27
  410.3 70.0 %collective-permute-done.4 = f32[6,384,384]{2,1,0:T(8,128)S(1)} collective-permute-done((f32[6,384,384]{2,1,0:T(8,128)S(1)}, f32[6,384,384]{2,1,0:T(8,128)S(1)}, u32[]{:S(2)}, u32[]{:S(2)}) %collective-permute-start.4) | collective-permute-done | bytes 3538976 | tf_op jit(solution)/shard_map/ppermute | solution.py:27
  480.3 4.6 add_add_fusion
  (173 shorter events, 85.2 us)
Async XLA Ops:
  1.4 12.3 %copy-start.1 = (f32[6,384]{1,0:T(8,128)S(1)}, f32[6,384]{1,0:T(8,128)}, u32[]{:S(2)}) copy-start(f32[6,384]{1,0:T(8,128)} %param.10) | copy-start | bytes 27652
  1.4 12.3 %copy-start.3 = (f32[6]{0:T(128)S(1)}, f32[6]{0:T(128)}, u32[]{:S(2)}) copy-start(f32[6]{0:T(128)} %param.11) | copy-start | bytes 76
  1.4 18.0 %copy-start.2 = (s32[16,2]{0,1:T(2,128)S(1)}, s32[16,2]{0,1:T(2,128)}, u32[]{:S(2)}) copy-start(s32[16,2]{0,1:T(2,128)} %param.13) | copy-start | bytes 388
  8.0 157.3 %collective-permute-start.1 = (bf16[6,1536,384]{2,1,0:T(8,128)(2,1)}, bf16[6,1536,384]{2,1,0:T(8,128)(2,1)}, u32[]{:S(2)}, u32[]{:S(2)}) collective-permute-start(bf16[6,1536,384]{2,1,0:T(8,128)(2,1)} %broadcast_select_fusion), channel_id=1, source_target_pairs={{1,0},{2,1},{3,2},{4,3},{5,4},{6,5},{7,6},{8,7},{9,8},{10,9},{11,1... | collective-permute-start | bytes 21233672 | tf_op jit(solution)/shard_map/ppermute | solution.py:19
  10.6 154.7 %collective-permute-start = (bf16[6,1536,384]{2,1,0:T(8,128)(2,1)}, bf16[6,1536,384]{2,1,0:T(8,128)(2,1)}, u32[]{:S(2)}, u32[]{:S(2)}) collective-permute-start(bf16[6,1536,384]{2,1,0:T(8,128)(2,1)} %broadcast_select_fusion), channel_id=1, source_target_pairs={{0,1},{1,2},{2,3},{3,4},{4,5},{5,6},{6,7},{7,8},{8,9},{9,10},{10,1... | collective-permute-start | bytes 21233672 | tf_op jit(solution)/shard_map/ppermute | solution.py:18
  13.8 151.4 %collective-permute-start.3 = (f32[6,384]{1,0:T(8,128)S(1)}, f32[6,384]{1,0:T(8,128)S(1)}, u32[]{:S(2)}, u32[]{:S(2)}) collective-permute-start(f32[6,384]{1,0:T(8,128)S(1)} %broadcast_subtract_fusion), channel_id=1, source_target_pairs={{1,0},{2,1},{3,2},{4,3},{5,4},{6,5},{7,6},{8,7},{9,8},{10,9},{11,1... | collective-permute-start | bytes 27656 | tf_op jit(solution)/shard_map/ppermute | solution.py:19
  15.7 149.6 %collective-permute-start.2 = (f32[6,384]{1,0:T(8,128)S(1)}, f32[6,384]{1,0:T(8,128)S(1)}, u32[]{:S(2)}, u32[]{:S(2)}) collective-permute-start(f32[6,384]{1,0:T(8,128)S(1)} %broadcast_subtract_fusion), channel_id=1, source_target_pairs={{0,1},{1,2},{2,3},{3,4},{4,5},{5,6},{6,7},{7,8},{8,9},{9,10},{10,1... | collective-permute-start | bytes 27656 | tf_op jit(solution)/shard_map/ppermute | solution.py:18
  332.2 3.7 copy-start.4
  332.2 148.1 %copy-start = (f32[6,384,384]{2,1,0:T(8,128)S(1)}, f32[6,384,384]{2,1,0:T(8,128)}, u32[]{:S(2)}) copy-start(f32[6,384,384]{2,1,0:T(8,128)} %get-tuple-element.68) | copy-start | bytes 10616836
  335.9 144.4 %collective-permute-start.4 = (f32[6,384,384]{2,1,0:T(8,128)S(1)}, f32[6,384,384]{2,1,0:T(8,128)S(1)}, u32[]{:S(2)}, u32[]{:S(2)}) collective-permute-start(f32[6,384,384]{2,1,0:T(8,128)S(1)} %get-tuple-element.107), channel_id=1, source_target_pairs={{1,0},{2,1},{3,2},{4,3},{5,4},{6,5},{7,6},{8,7},{9,8},{10,9},{11,1... | collective-permute-start | bytes 10616840 | tf_op jit(solution)/shard_map/ppermute | solution.py:27
  337.8 142.5 %collective-permute-start.5 = (f32[6,384,384]{2,1,0:T(8,128)S(1)}, f32[6,384,384]{2,1,0:T(8,128)S(1)}, u32[]{:S(2)}, u32[]{:S(2)}) collective-permute-start(f32[6,384,384]{2,1,0:T(8,128)S(1)} %get-tuple-element.108), channel_id=1, source_target_pairs={{0,1},{1,2},{2,3},{3,4},{4,5},{5,6},{6,7},{7,8},{8,9},{9,10},{10,1... | collective-permute-start | bytes 10616840 | tf_op jit(solution)/shard_map/ppermute | solution.py:27
where the time goes:
time: 481 us; the launch traced here: 485 us
  waiting for transfers between devices  216 us (45%)
  starting transfers between devices  85.6 us (18%)
  local copies, waits for them, and re-layouts  63.5 us (13%)
  other arithmetic  49.7 us (10%)
  loops' own time  44.1 us (9%)
  matrix products  25.5 us (5%)
    ppermute x2, waiting for transfers between devices, extended(): after = lax.ppermute(leading, axis, down)  146 us
    ppermute x2, starting transfers between devices, from_behind(): return lax.ppermute(block, axis, route)  74.4 us
    ppermute x2, waiting for transfers between devices, from_behind(): return lax.ppermute(block, axis, route)  70 us
    dynamic_slice x38, local copies, waits for them, and re-layouts, take_row(): return lax.dynamic_index_in_dim(stack, where, 0, keepdims=False)  35.6 us
    another operation x1, loops' own time, per_device(): lax.scan(pair_step, (own, window_acc), pairs)  31.9 us
    concatenate x2, other arithmetic, extended(): x = jnp.concatenate([before, x, after], axis=dim)  19.6 us
    dot_general x6, matrix products, pair_work(): lax.dot_general(left_block, right_block, (((0,), (0,)), ((), ())), prefer...  18.9 us
    dynamic_update_slice x16, other arithmetic, add_row(): lax.dynamic_update_index_in_dim(stack, take_row(stack, where) + term, whe...  18 us
  transfers between devices with their start and end apart: 6, of which 3 were waited for; matrix products, arithmetic and copies ran while one was open for 0% of the time, Pallas kernels for 0%

commit v1 on v0

v1 whole, which is shorter than its diff:
```python
import functools
import math

import jax
import jax.numpy as jnp
from jax import lax
from jax.experimental import pallas as pl
from jax.experimental.pallas import tpu as pltpu
from jax.sharding import PartitionSpec as P

GRAIN = 128
MESH = pl.DeviceIdType.MESH
NT = (((1,), (1,)), ((), ()))
TN = (((0,), (0,)), ((), ()))
WINDOW = 6


def kernel(
    size, n, aux, width, factor,
    blocks, info, wself, wleft,
    dens, eself, eleft, eright,
    own, got, left_t, linfo, own_col, left_col, acc, ret_out, ret_in, ein,
    own_sem, blk_send, blk_recv, info_sem, ret_send, ret_recv, e_send, e_recv,
):
    me = lax.axis_index("orb")
    has_left = me > 0
    has_right = me < size - 1
    right = jnp.minimum(me + 1, size - 1)
    left = jnp.maximum(me - 1, 0)
    reach = n // 2

    barrier = pltpu.get_barrier_semaphore()

    @pl.when(has_left)
    def _():
        pl.semaphore_signal(barrier, inc=1, device_id={"orb": left}, device_id_type=MESH)

    @pl.when(has_right)
    def _():
        pl.semaphore_signal(barrier, inc=1, device_id={"orb": right}, device_id_type=MESH)

    def own_copy(k):
        return pltpu.make_async_copy(blocks.at[k], own.at[k], own_sem.at[k])

    def blk_copy(k):
        return pltpu.make_async_remote_copy(
            src_ref=blocks.at[k], dst_ref=got.at[k], send_sem=blk_send.at[k], recv_sem=blk_recv.at[k],
            device_id={"orb": right}, device_id_type=MESH,
        )

    def info_copy():
        return pltpu.make_async_remote_copy(
            src_ref=info, dst_ref=linfo, send_sem=info_sem.at[0], recv_sem=info_sem.at[1],
            device_id={"orb": right}, device_id_type=MESH,
        )

    def ret_copy(k):
        return pltpu.make_async_remote_copy(
            src_ref=ret_out.at[k], dst_ref=ret_in.at[k], send_sem=ret_send.at[k], recv_sem=ret_recv.at[k],
            device_id={"orb": left}, device_id_type=MESH,
        )

    def e_copy(k):
        return pltpu.make_async_remote_copy(
            src_ref=eleft.at[pl.ds(k * n, n)], dst_ref=ein.at[pl.ds(k * n, n)],
            send_sem=e_send.at[k], recv_sem=e_recv.at[k],
            device_id={"orb": left}, device_id_type=MESH,
        )

    for k in range(n):
        own_copy(k).start()

    peers = has_left.astype(jnp.int32) + has_right.astype(jnp.int32)
    pl.semaphore_wait(barrier, peers)

    @pl.when(has_right)
    def _():
        info_copy().start()
        for k in range(min(WINDOW, n)):
            blk_copy(k).start()

    def columns(source, target):
        turned = jnp.transpose(source[0:8, :])
        for k in range(n):
            target[k] = jnp.broadcast_to(turned[:, k : k + 1], (width, GRAIN))

    columns(info, own_col)
    dens[...] = jnp.zeros_like(dens)

    @pl.loop(0, n)
    def _(k):
        own_copy(k).wait()
        own[k] = own[k] * info[pl.ds(8 + k, 1), :].astype(jnp.bfloat16)

    def product(col, r, w):
        exchange = jnp.dot(left_t[...], own[r], preferred_element_type=jnp.float32)
        denom = jnp.concatenate([col] * (width // GRAIN), axis=1) + info[pl.ds(r, 1), :]
        amplitude = -exchange / denom
        parts = jnp.sum((exchange * amplitude).reshape(width // 8, 8, width), axis=0)
        energy = parts[:, :GRAIN]
        for c in range(1, width // GRAIN):
            energy = energy + parts[:, c * GRAIN : (c + 1) * GRAIN]
        rounded = amplitude.astype(jnp.bfloat16)
        first = lax.dot_general(rounded, rounded, NT, preferred_element_type=jnp.float32)
        second = lax.dot_general(rounded, rounded, TN, preferred_element_type=jnp.float32)
        scale = w * factor
        dens[r] += second * scale
        return energy, first * scale

    @pl.loop(0, n)
    def _(i):
        left_t[...] = jnp.transpose(own[i])
        total = None
        for t in range(1, reach + 1):
            at = i * reach + (t - 1)
            energy, first = product(own_col[i], lax.rem(i + t, n), wself[pl.ds(at, 1), :])
            eself[at] = energy
            total = first if total is None else total + first
        dens[i] += total

    @pl.when(has_left)
    def _():
        info_copy().wait_recv()
        columns(linfo, left_col)

    step = 2 if n % 2 == 0 else 1

    @pl.loop(0, n)
    def _(k):
        @pl.when(has_left)
        def _():
            blk_copy(k).wait_recv()
            left_t[...] = jnp.transpose(got[k] * linfo[pl.ds(8 + k, 1), :].astype(jnp.bfloat16))
            acc[...] = jnp.zeros_like(acc)

            @pl.loop(0, n // step)
            def _(q):
                total = None
                for s in range(step):
                    r = q * step + s
                    at = k * n + r
                    w = linfo[pl.ds(16 + at, 1), :] + wleft[pl.ds(at, 1), :]
                    energy, first = product(left_col[k], r, w)
                    eleft[at] = energy
                    total = first if total is None else total + first
                acc[...] += total

            ret_out[k] = acc[...].astype(jnp.bfloat16)
            ret_copy(k).start()
            e_copy(k).start()

        if WINDOW < n:
            @pl.when(has_right & (k + WINDOW < n))
            def _():
                blk_copy(k).wait_send()
                blk_copy(k + WINDOW).start()

    @pl.when(has_right)
    def _():
        info_copy().wait_send()

        @pl.loop(max(n - WINDOW, 0), n)
        def _(k):
            blk_copy(k).wait_send()

        @pl.loop(0, n)
        def _(k):
            ret_copy(k).wait_recv()
            dens[k] += ret_in[k].astype(jnp.float32)
            e_copy(k).wait_recv()

        eright[...] = ein[...]

    @pl.when(has_left)
    def _():
        @pl.loop(0, n)
        def _(k):
            ret_copy(k).wait_send()
            e_copy(k).wait_send()

    @pl.when(jnp.logical_not(has_right))
    def _():
        eright[...] = jnp.zeros_like(eright)

    @pl.when(jnp.logical_not(has_left))
    def _():
        eleft[...] = jnp.zeros_like(eleft)


def per_device(blocks, pao_energy, occ_energy, dom_blocks, pairs):
    n, aux, width = blocks.shape
    size = lax.axis_size("orb")
    reach = n // 2
    factor = 1.0 / math.sqrt(width)
    start = lax.axis_index("orb") * n
    column = lax.broadcasted_iota(jnp.int32, (n, width), 1)
    live_cols = (column < (dom_blocks * GRAIN)[:, None]).astype(jnp.float32)
    shifted = pao_energy - occ_energy[:, None]

    live = pairs[:, 0] >= 0
    i = pairs[:, 0] - start
    j = pairs[:, 1] - start
    side = jnp.where(j < 0, 0, jnp.where(j >= n, 2, 1))
    ahead = jnp.mod(j - i, n)
    near = (ahead < n - ahead) | ((2 * ahead == n) & (i < j))
    self_at = jnp.where(near, i * reach + ahead - 1, j * reach + (n - ahead) - 1)
    n_self = n * reach
    at = jnp.where(
        side == 1, self_at,
        jnp.where(side == 0, n_self + (j + n) * n + i, n_self + n * n + i * n + (j - n)),
    )
    hot = ((at[:, None] == jnp.arange(n_self + 2 * n * n)[None, :]) & live[:, None]).astype(jnp.float32)
    weight = jnp.broadcast_to(jnp.sum(hot, axis=0)[:, None], (hot.shape[1], width))
    pad = jnp.zeros((8 - n, width), jnp.float32)
    info = jnp.concatenate([shifted, pad, live_cols, pad, weight[n_self + n * n :]], axis=0)
    wself = weight[:n_self]
    wleft = weight[n_self : n_self + n * n]

    f32, bf16 = jnp.float32, jnp.bfloat16
    vmem = pl.BlockSpec(memory_space=pltpu.VMEM)
    dens, eself, eleft, eright = pl.pallas_call(
        functools.partial(kernel, size, n, aux, width, factor),
        out_shape=(
            jax.ShapeDtypeStruct((n, width, width), f32),
            jax.ShapeDtypeStruct((n_self, 8, GRAIN), f32),
            jax.ShapeDtypeStruct((n * n, 8, GRAIN), f32),
            jax.ShapeDtypeStruct((n * n, 8, GRAIN), f32),
        ),
        in_specs=[pl.BlockSpec(memory_space=pl.ANY), vmem, vmem, vmem],
        out_specs=(vmem, vmem, vmem, vmem),
        scratch_shapes=[
            pltpu.VMEM((n, aux, width), bf16),
            pltpu.VMEM((n, aux, width), bf16),
            pltpu.VMEM((width, aux), bf16),
            pltpu.VMEM(info.shape, f32),
            pltpu.VMEM((n, width, GRAIN), f32),
            pltpu.VMEM((n, width, GRAIN), f32),
            pltpu.VMEM((width, width), f32),
            pltpu.VMEM((n, width, width), bf16),
            pltpu.VMEM((n, width, width), bf16),
            pltpu.VMEM((n * n, 8, GRAIN), f32),
            pltpu.SemaphoreType.DMA((n,)),
            pltpu.SemaphoreType.DMA((n,)),
            pltpu.SemaphoreType.DMA((n,)),
            pltpu.SemaphoreType.DMA((2,)),
            pltpu.SemaphoreType.DMA((n,)),
            pltpu.SemaphoreType.DMA((n,)),
            pltpu.SemaphoreType.DMA((n,)),
            pltpu.SemaphoreType.DMA((n,)),
        ],
        compiler_params=pltpu.CompilerParams(
            collective_id=0, has_side_effects=True, vmem_limit_bytes=52 * 1024 * 1024
        ),
    )(blocks, info, wself, wleft)

    table = jnp.concatenate([jnp.sum(e, axis=(1, 2)) for e in (eself, eleft, eright)])
    energies = 2.0 * jnp.sum(jnp.where(hot > 0, table[None, :], 0.0), axis=1)
    return (energies, dens)


def solution(mesh):
    in_specs = (
        P(("groups", "orb"), None, None),
        P(("groups", "orb"), None),
        P(("groups", "orb")),
        P(("groups", "orb")),
        P(("groups", "orb"), None),
    )
    out_specs = (P(("groups", "orb")), P(("groups", "orb"), None, None))
    return jax.shard_map(
        per_device, mesh=mesh, in_specs=in_specs, out_specs=out_specs, check_vma=False
    )
```

time: 481 us -> 127 us (0.26)
  waiting for transfers between devices: 216 us -> 0 us
  Pallas kernels: 0 us -> 117 us
  starting transfers between devices: 85.6 us -> 0 us
  local copies, waits for them, and re-layouts: 63.5 us -> 4.35 us
  other arithmetic: 49.7 us -> 4.75 us
  loops' own time: 44.1 us -> 0 us
  matrix products: 25.5 us -> 0 us
    ppermute x6 -> x0, waiting for transfers between devices: 216 us -> none  [the longest x2 146 us: extended(): after = lax.ppermute(leading, axis, down)]
    pallas_call x0 -> x1, Pallas kernels: none -> 117 us  [per_device(): pl.pallas_call(functools.partial(kernel, size, n, aux, width, factor), ou...]
    ppermute x6 -> x0, starting transfers between devices: 85.6 us -> none  [the longest x2 74.4 us: from_behind(): return lax.ppermute(block, axis, route)]
    another operation x17 -> x0, loops' own time: 44.1 us -> none  [the longest x1 31.9 us: per_device(): lax.scan(pair_step, (own, window_acc), pairs)]
    dynamic_slice x54 -> x0, local copies, waits for them, and re-layouts: 35.7 us -> none  [the longest x38 35.6 us: take_row(): return lax.dynamic_index_in_dim(stack, where, 0, keepdims=False)]
    dot_general x18 -> x0, matrix products: 25.5 us -> none  [the longest x6 18.9 us: pair_work(): lax.dot_general(left_block, right_block, (((0,), (0,)), ((), ())), prefer...]
    concatenate x2 -> x1, other arithmetic: 19.6 us -> 0.08 us  [per_device(): jnp.concatenate([jnp.sum(e, axis=(1, 2)) for e in (eself, eleft, eright)])]
    dynamic_update_slice x16 -> x0, other arithmetic: 18 us -> none  [add_row(): lax.dynamic_update_index_in_dim(stack, take_row(stack, where) + term, whe...]
  transfers between devices with their start and end apart: 6 -> 0, of which waited for: 3 -> 0; matrix products, arithmetic and copies ran while one was open for 0% -> 0% of each run, Pallas kernels for 0% -> 0%
where the time goes in v1:
time: 127 us; the launch traced here: 126 us
  Pallas kernels  117 us (92%)
  other arithmetic  4.75 us (4%)
  local copies, waits for them, and re-layouts  4.35 us (3%)
    pallas_call x1, Pallas kernels, per_device(): pl.pallas_call(functools.partial(kernel, size, n, aux, width, factor), ou...  117 us
    unnamed x1, local copies, waits for them, and re-layouts  4.02 us

profile of v1, /device:TPU:9, one launch (start us, length us, event | category | flops | bytes accessed | tf_op | source)
XLA Modules:
  0.0 126.3 jit_solution(17634349040148154118)
XLA Ops:
  0.6 0.8 fusion.3
  1.4 0.7 compare_bitcast_fusion
  2.1 0.1 convert_reduce_fusion
  2.2 0.7 broadcast_multiply_fusion.1
  2.8 0.1 fusion.4
  2.9 0.1 fusion
  3.0 0.8 broadcast_subtract_fusion
  3.8 0.1 broadcast_in_dim.43.wself
  3.8 0.1 broadcast_in_dim.44.wleft
  3.9 0.1 broadcast_in_dim.42
  4.0 116.5 %shard_map.68 = (f32[6,384,384]{2,1,0:T(8,128)}, f32[18,8,128]{2,1,0:T(8,128)S(1)}, f32[36,8,128]{2,1,0:T(8,128)S(1)}, f32[36,8,128]{2,1,0:T(8,128)S(1)}) custom-call(bf16[6,1536,384]{2,1,0:T(8,128)(2,1)} %blocks.1, f32[52,384]{1,0:T(8,128)S(1)} %concatenate.6.info, f32[18,384]{1,0:T(8,128)S(1)} %broadcast_in_dim.43.wself, f32[36,384]{1,0:T(8,128)S(1)} %broadcast_in_dim.44.wleft), custom_call_target="tpu_custom_call" | custom-call | tf_op jit(solution)/shard_map/pallas_call | solution.py:221
  120.5 0.2 reduce_sum.46
  120.8 0.3 reduce_sum.47
  121.1 0.3 reduce_sum.48
  121.5 0.1 pad_maximum_fusion
  121.5 0.2 select_reduce_fusion
  121.7 0.5 broadcast_multiply_fusion
  122.2 4.0 %copy.8 = f32[6,384,384]{2,1,0:T(8,128)} copy(f32[6,384,384]{2,1,0:T(8,128)} %get-tuple-element.15) | data formatting | bytes 7077888
  (2 shorter events, 0.0 us)

commit v2 on v1

v2 whole, which is shorter than its diff:
```python
import functools
import math

import jax
import jax.numpy as jnp
from jax import lax
from jax.experimental import pallas as pl
from jax.experimental.pallas import tpu as pltpu
from jax.sharding import PartitionSpec as P

GRAIN = 128
MESH = pl.DeviceIdType.MESH
NT = (((1,), (1,)), ((), ()))
TN = (((0,), (0,)), ((), ()))


def kernel(
    size, factor,
    blocks, pao, occ, dom, pairs,
    dens, energies,
    own, got, left_t, info, linfo, wtab, wright, own_col, left_col, acc, ret_out, ret_in, etab, ein,
    own_sem, blk_send, blk_recv, info_sem, w_sem, ret_send, ret_recv, e_sem,
):
    n, _, width = blocks.shape
    tiles = width // GRAIN
    reach = n // 2
    edge = wright.shape[0]
    at_left, at_self = edge, 2 * edge
    me = lax.axis_index("orb")
    has_left = me > 0
    has_right = me < size - 1
    right = jnp.minimum(me + 1, size - 1)
    left = jnp.maximum(me - 1, 0)

    barrier = pltpu.get_barrier_semaphore()

    @pl.when(has_left)
    def _():
        pl.semaphore_signal(barrier, inc=1, device_id={"orb": left}, device_id_type=MESH)

    @pl.when(has_right)
    def _():
        pl.semaphore_signal(barrier, inc=1, device_id={"orb": right}, device_id_type=MESH)

    def own_copy(k):
        return pltpu.make_async_copy(blocks.at[k], own.at[k], own_sem.at[k])

    def to_right(source, target, send_sem, recv_sem):
        return pltpu.make_async_remote_copy(
            src_ref=source, dst_ref=target, send_sem=send_sem, recv_sem=recv_sem,
            device_id={"orb": right}, device_id_type=MESH,
        )

    def to_left(source, target, send_sem, recv_sem):
        return pltpu.make_async_remote_copy(
            src_ref=source, dst_ref=target, send_sem=send_sem, recv_sem=recv_sem,
            device_id={"orb": left}, device_id_type=MESH,
        )

    def blk_copy(k):
        return to_right(blocks.at[k], got.at[k], blk_send.at[k], blk_recv.at[k])

    def info_copy():
        return to_right(info, linfo, info_sem.at[0], info_sem.at[1])

    def w_copy():
        return to_right(wtab.at[pl.ds(0, edge)], wright, w_sem.at[0], w_sem.at[1])

    def ret_copy(k):
        return to_left(ret_out.at[k], ret_in.at[k], ret_send.at[k], ret_recv.at[k])

    def e_copy():
        return to_left(etab.at[pl.ds(at_left, edge)], ein, e_sem.at[0], e_sem.at[1])

    for k in range(n):
        own_copy(k).start()

    info[...] = jnp.zeros_like(info)
    column = lax.broadcasted_iota(jnp.int32, (1, width), 1)
    for k in range(n):
        info[k : k + 1, :] = pao[k : k + 1, :] - occ[k]
        info[8 + k : 9 + k, :] = jnp.where(column < dom[k] * GRAIN, 1.0, 0.0)

    start = me * n
    live = pairs[:, 0:1] >= 0
    i = pairs[:, 0:1] - start
    j = pairs[:, 1:2] - start
    ahead = jnp.where(j < i, j - i + n, j - i)
    near = (ahead < n - ahead) | ((2 * ahead == n) & (i < j))
    place = at_self + jnp.where(near, i * reach + ahead - 1, j * reach + (n - ahead) - 1)
    place = jnp.where(j < 0, at_left + (j + n) * n + i, place)
    place = jnp.where(j >= n, i * n + (j - n), place)
    place = jnp.where(live, place, -1)
    spots = lax.broadcasted_iota(jnp.int32, (pairs.shape[0], GRAIN), 1)
    hot = jnp.where(place == spots, 1.0, 0.0)
    counts = jnp.sum(hot, axis=0, keepdims=True)
    wtab[...] = jnp.transpose(jnp.broadcast_to(counts, (GRAIN, GRAIN)))

    peers = has_left.astype(jnp.int32) + has_right.astype(jnp.int32)
    pl.semaphore_wait(barrier, peers)

    @pl.when(has_right)
    def _():
        info_copy().start()
        w_copy().start()
        for k in range(n):
            blk_copy(k).start()

    def columns(source, target):
        turned = jnp.transpose(source[0:8, :])
        for k in range(n):
            target[k] = jnp.broadcast_to(turned[:, k : k + 1], (width, GRAIN))

    def wide(x):
        return jnp.concatenate([x] * tiles, axis=1)

    columns(info, own_col)
    dens[...] = jnp.zeros_like(dens)
    etab[...] = jnp.zeros_like(etab)

    @pl.loop(0, n)
    def _(k):
        own_copy(k).wait()
        own[k] = own[k] * info[pl.ds(8 + k, 1), :].astype(jnp.bfloat16)

    def product(col, r, w, spot):
        exchange = jnp.dot(left_t[...], own[r], preferred_element_type=jnp.float32)
        denom = wide(col) + info[pl.ds(r, 1), :]
        amplitude = -exchange / denom
        parts = jnp.sum((exchange * amplitude).reshape(width // 8, 8, width), axis=0)
        energy = parts[:, :GRAIN]
        for c in range(1, tiles):
            energy = energy + parts[:, c * GRAIN : (c + 1) * GRAIN]
        etab[pl.ds(spot, 1), :] = jnp.sum(energy, axis=0, keepdims=True)
        rounded = amplitude.astype(jnp.bfloat16)
        first = lax.dot_general(rounded, rounded, NT, preferred_element_type=jnp.float32)
        second = lax.dot_general(rounded, rounded, TN, preferred_element_type=jnp.float32)
        scale = wide(w) * factor
        dens[r] += second * scale
        return first * scale

    @pl.loop(0, n)
    def _(i):
        left_t[...] = jnp.transpose(own[i])
        total = None
        for t in range(1, reach + 1):
            spot = at_self + i * reach + (t - 1)
            first = product(own_col[i], lax.rem(i + t, n), wtab[pl.ds(spot, 1), :], spot)
            total = first if total is None else total + first
        dens[i] += total

    upper = [(a, b) for a in range(tiles) for b in range(a, tiles)]
    step = 2 if n % 2 == 0 else 1

    @pl.when(has_left)
    def _():
        info_copy().wait_recv()
        w_copy().wait_recv()
        columns(linfo, left_col)

        @pl.loop(0, n)
        def _(k):
            blk_copy(k).wait_recv()

            @pl.when(k == n - 1)
            def _():
                @pl.loop(0, n - 1)
                def _(m):
                    ret_copy(m).start()

            left_t[...] = jnp.transpose(got[k] * linfo[pl.ds(8 + k, 1), :].astype(jnp.bfloat16))
            acc[...] = jnp.zeros_like(acc)

            @pl.loop(0, n // step)
            def _(q):
                total = None
                for s in range(step):
                    r = q * step + s
                    at = k * n + r
                    w = wright[pl.ds(at, 1), :] + wtab[pl.ds(at_left + at, 1), :]
                    first = product(left_col[k], r, w, at_left + at)
                    total = first if total is None else total + first
                acc[...] += total

            for u, (a, b) in enumerate(upper):
                ret_out[k, u] = acc[a * GRAIN : (a + 1) * GRAIN, b * GRAIN : (b + 1) * GRAIN].astype(jnp.bfloat16)

        ret_copy(n - 1).start()
        e_copy().start()

    @pl.when(has_right)
    def _():
        info_copy().wait_send()
        w_copy().wait_send()

        @pl.loop(0, n)
        def _(k):
            blk_copy(k).wait_send()

        @pl.loop(0, n)
        def _(k):
            ret_copy(k).wait_recv()
            for u, (a, b) in enumerate(upper):
                rows, cols = pl.ds(a * GRAIN, GRAIN), pl.ds(b * GRAIN, GRAIN)
                term = ret_in[k, u].astype(jnp.float32)
                dens[k, rows, cols] += term
                if a != b:
                    dens[k, cols, rows] += jnp.transpose(term)

        e_copy().wait_recv()
        etab[0:edge, :] = ein[...]

    table = jnp.sum(jnp.transpose(etab[...]), axis=0, keepdims=True)
    energies[...] = 2.0 * jnp.sum(hot * table, axis=1, keepdims=True)

    @pl.when(has_left)
    def _():
        e_copy().wait_send()

        @pl.loop(0, n)
        def _(k):
            ret_copy(k).wait_send()


def per_device(blocks, pao_energy, occ_energy, dom_blocks, pairs):
    n, aux, width = blocks.shape
    size = lax.axis_size("orb")
    factor = 1.0 / math.sqrt(width)
    edge = -(-n * n // 8) * 8
    tiles = width // GRAIN
    upper = tiles * (tiles + 1) // 2
    f32, bf16 = jnp.float32, jnp.bfloat16
    vmem = pl.BlockSpec(memory_space=pltpu.VMEM)
    smem = pl.BlockSpec(memory_space=pltpu.SMEM)
    many = pltpu.SemaphoreType.DMA((n,))
    two = pltpu.SemaphoreType.DMA((2,))
    dens, energies = pl.pallas_call(
        functools.partial(kernel, size, factor),
        out_shape=(
            jax.ShapeDtypeStruct((n, width, width), f32),
            jax.ShapeDtypeStruct((pairs.shape[0], 1), f32),
        ),
        in_specs=[pl.BlockSpec(memory_space=pl.ANY), vmem, smem, smem, vmem],
        out_specs=(vmem, vmem),
        scratch_shapes=[
            pltpu.VMEM((n, aux, width), bf16),
            pltpu.VMEM((n, aux, width), bf16),
            pltpu.VMEM((width, aux), bf16),
            pltpu.VMEM((16, width), f32),
            pltpu.VMEM((16, width), f32),
            pltpu.VMEM((GRAIN, GRAIN), f32),
            pltpu.VMEM((edge, GRAIN), f32),
            pltpu.VMEM((n, width, GRAIN), f32),
            pltpu.VMEM((n, width, GRAIN), f32),
            pltpu.VMEM((width, width), f32),
            pltpu.VMEM((n, upper, GRAIN, GRAIN), bf16),
            pltpu.VMEM((n, upper, GRAIN, GRAIN), bf16),
            pltpu.VMEM((GRAIN, GRAIN), f32),
            pltpu.VMEM((edge, GRAIN), f32),
            many, many, many, two, two, many, many, two,
        ],
        compiler_params=pltpu.CompilerParams(
            collective_id=0, has_side_effects=True, vmem_limit_bytes=52 * 1024 * 1024
        ),
    )(blocks, pao_energy, occ_energy, dom_blocks, pairs)
    return (energies[:, 0], dens)


def solution(mesh):
    in_specs = (
        P(("groups", "orb"), None, None),
        P(("groups", "orb"), None),
        P(("groups", "orb")),
        P(("groups", "orb")),
        P(("groups", "orb"), None),
    )
    out_specs = (P(("groups", "orb")), P(("groups", "orb"), None, None))
    return jax.shard_map(
        per_device, mesh=mesh, in_specs=in_specs, out_specs=out_specs, check_vma=False
    )
```

time: 127 us -> 107 us (0.84)
  Pallas kernels: 117 us -> 98 us
  other arithmetic: 4.75 us -> 0.63 us
  local copies, waits for them, and re-layouts: 4.35 us -> 6.79 us
    pallas_call x1, Pallas kernels: 117 us -> 98 us  [per_device(): pl.pallas_call(functools.partial(kernel, size, factor), out_shape=(jax.Sh...]
    unnamed x1 -> x8, local copies, waits for them, and re-layouts: 4.02 us -> 6.79 us
where the time goes in v2:
time: 107 us; the launch traced here: 106 us
  Pallas kernels  98 us (92%)
  local copies, waits for them, and re-layouts  6.79 us (6%)
    pallas_call x1, Pallas kernels, per_device(): pl.pallas_call(functools.partial(kernel, size, factor), out_shape=(jax.Sh...  98 us
    unnamed x8, local copies, waits for them, and re-layouts  6.79 us

profile of v2, /device:TPU:9, one launch (start us, length us, event | category | flops | bytes accessed | tf_op | source)
XLA Modules:
  0.0 106.1 jit_solution(3807193571607351607)
XLA Ops:
  0.6 0.8 copy.8.pairs
  1.4 0.0 copy-start
  1.4 0.7 copy-done
  2.1 0.0 copy-start.1
  2.1 0.7 copy-done.1
  2.7 0.0 copy-start.2
  2.8 0.7 copy-done.2
  3.4 98.0 %shard_map.68 = (f32[6,384,384]{2,1,0:T(8,128)}, f32[16,1]{1,0:T(8,128)S(1)}) custom-call(bf16[6,1536,384]{2,1,0:T(8,128)(2,1)} %blocks.1, f32[6,384]{1,0:T(8,128)S(1)} %copy-done, f32[6]{0:T(128)S(1)} %copy-done.1, s32[6]{0:T(128)S(1)} %copy-done.2, s32[16,2]{1,0:T(8,128)S(1)} %copy.8.pairs), custom_call_target="tpu_custom_call" | custom-call | tf_op jit(solution)/shard_map/pallas_call | solution.py:237
  101.5 0.6 reduce
  102.1 4.0 %copy.10 = f32[6,384,384]{2,1,0:T(8,128)} copy(f32[6,384,384]{2,1,0:T(8,128)} %get-tuple-element.9) | data formatting | bytes 7077888
Async XLA Ops:
  1.4 0.7 copy-start
  2.1 0.7 copy-start.1
  2.7 0.7 copy-start.2

commit v3 on v2

--- a/solution.py
+++ b/solution.py
@@ -16,10 +16,11 @@
 
 def kernel(
     size, factor,
-    blocks, pao, occ, dom, pairs,
-    dens, energies,
-    own, got, left_t, info, linfo, wtab, wright, own_col, left_col, acc, ret_out, ret_in, etab, ein,
-    own_sem, blk_send, blk_recv, info_sem, w_sem, ret_send, ret_recv, e_sem,
+    blocks, pao_hbm, occ_hbm, dom_hbm, pairs_hbm,
+    part, ret_in, energies,
+    pao, occ, dom, pairs,
+    own, got, left_t, info, linfo, wtab, wright, own_col, left_col, acc, ret_out, etab, ein, dens,
+    small_sem, own_sem, blk_send, blk_recv, info_sem, w_sem, ret_send, ret_recv, e_sem, part_sem,
 ):
     n, _, width = blocks.shape
     tiles = width // GRAIN
@@ -72,8 +73,25 @@
     def e_copy():
         return to_left(etab.at[pl.ds(at_left, edge)], ein, e_sem.at[0], e_sem.at[1])
 
+    small = [
+        pltpu.make_async_copy(source, target, small_sem.at[at])
+        for at, (source, target) in enumerate(
+            ((pao_hbm, pao), (occ_hbm, occ), (dom_hbm, dom), (pairs_hbm, pairs))
+        )
+    ]
+    for copy in small:
+        copy.start()
+    peers = has_left.astype(jnp.int32) + has_right.astype(jnp.int32)
+    pl.semaphore_wait(barrier, peers)
+
+    @pl.when(has_right)
+    def _():
+        blk_copy(0).start()
+
     for k in range(n):
         own_copy(k).start()
+    for copy in small:
+        copy.wait()
 
     info[...] = jnp.zeros_like(info)
     column = lax.broadcasted_iota(jnp.int32, (1, width), 1)
@@ -82,28 +100,25 @@
         info[8 + k : 9 + k, :] = jnp.where(column < dom[k] * GRAIN, 1.0, 0.0)
 
     start = me * n
-    live = pairs[:, 0:1] >= 0
-    i = pairs[:, 0:1] - start
-    j = pairs[:, 1:2] - start
+    live = pairs[0:1, :] >= 0
+    i = pairs[0:1, :] - start
+    j = pairs[1:2, :] - start
     ahead = jnp.where(j < i, j - i + n, j - i)
     near = (ahead < n - ahead) | ((2 * ahead == n) & (i < j))
     place = at_self + jnp.where(near, i * reach + ahead - 1, j * reach + (n - ahead) - 1)
     place = jnp.where(j < 0, at_left + (j + n) * n + i, place)
     place = jnp.where(j >= n, i * n + (j - n), place)
     place = jnp.where(live, place, -1)
-    spots = lax.broadcasted_iota(jnp.int32, (pairs.shape[0], GRAIN), 1)
+    spots = lax.broadcasted_iota(jnp.int32, (GRAIN, pairs.shape[1]), 0)
     hot = jnp.where(place == spots, 1.0, 0.0)
-    counts = jnp.sum(hot, axis=0, keepdims=True)
-    wtab[...] = jnp.transpose(jnp.broadcast_to(counts, (GRAIN, GRAIN)))
-
-    peers = has_left.astype(jnp.int32) + has_right.astype(jnp.int32)
-    pl.semaphore_wait(barrier, peers)
+    counts = jnp.sum(hot, axis=1, keepdims=True)
+    wtab[...] = jnp.broadcast_to(counts, (GRAIN, GRAIN))
 
     @pl.when(has_right)
     def _():
         info_copy().start()
         w_copy().start()
-        for k in range(n):
+        for k in range(1, n):
             blk_copy(k).start()
 
     def columns(source, target):
@@ -185,8 +200,14 @@
             for u, (a, b) in enumerate(upper):
                 ret_out[k, u] = acc[a * GRAIN : (a + 1) * GRAIN, b * GRAIN : (b + 1) * GRAIN].astype(jnp.bfloat16)
 
+        e_copy().start()
         ret_copy(n - 1).start()
-        e_copy().start()
+
+    def part_copy(k):
+        return pltpu.make_async_copy(dens.at[k], part.at[k], part_sem.at[k])
+
+    for k in range(n):
+        part_copy(k).start()
 
     @pl.when(has_right)
     def _():
@@ -197,29 +218,48 @@
         def _(k):
             blk_copy(k).wait_send()
 
+        e_copy().wait_recv()
+        etab[0:edge, :] = ein[...]
+
+    table = jnp.sum(etab[...], axis=1, keepdims=True)
+    energies[...] = 2.0 * jnp.sum(hot * table, axis=0, keepdims=True)
+
+    for k in range(n):
+        part_copy(k).wait()
+
+    @pl.when(has_left)
+    def _():
+        e_copy().wait_send()
+
+        @pl.loop(0, n)
+        def _(k):
+            ret_copy(k).wait_send()
+
+    @pl.when(has_right)
+    def _():
         @pl.loop(0, n)
         def _(k):
             ret_copy(k).wait_recv()
+
+
+def add_returned(size, part, ret, out):
+    tiles = part.shape[1] // GRAIN
+    upper = [(a, b) for a in range(tiles) for b in range(a, tiles)]
+    has_right = lax.axis_index("orb") < size - 1
+
+    @pl.when(has_right)
+    def _():
+        for k in range(part.shape[0]):
             for u, (a, b) in enumerate(upper):
                 rows, cols = pl.ds(a * GRAIN, GRAIN), pl.ds(b * GRAIN, GRAIN)
-                term = ret_in[k, u].astype(jnp.float32)
-                dens[k, rows, cols] += term
+                term = ret[k, u].astype(jnp.float32)
+                out[k, rows, cols] = part[k, rows, cols] + term
                 if a != b:
-                    dens[k, cols, rows] += jnp.transpose(term)
-
-        e_copy().wait_recv()
-        etab[0:edge, :] = ein[...]
-
-    table = jnp.sum(jnp.transpose(etab[...]), axis=0, keepdims=True)
-    energies[...] = 2.0 * jnp.sum(hot * table, axis=1, keepdims=True)
-
-    @pl.when(has_left)
-    def _():
-        e_copy().wait_send()
-
-        @pl.loop(0, n)
-        def _(k):
-            ret_copy(k).wait_send()
+                    out[k, cols, rows] = part[k, cols, rows] + jnp.transpose(term)
+
+    @pl.when(jnp.logical_not(has_right))
+    def _():
+        out[...] = part[...]
 
 
 def per_device(blocks, pao_energy, occ_energy, dom_blocks, pairs):
@@ -231,18 +271,24 @@
     upper = tiles * (tiles + 1) // 2
     f32, bf16 = jnp.float32, jnp.bfloat16
     vmem = pl.BlockSpec(memory_space=pltpu.VMEM)
-    smem = pl.BlockSpec(memory_space=pltpu.SMEM)
+    hbm = pl.BlockSpec(memory_space=pl.ANY)
     many = pltpu.SemaphoreType.DMA((n,))
     two = pltpu.SemaphoreType.DMA((2,))
-    dens, energies = pl.pallas_call(
+    slots = pairs.shape[0]
+    part, ret, energies = pl.pallas_call(
         functools.partial(kernel, size, factor),
         out_shape=(
             jax.ShapeDtypeStruct((n, width, width), f32),
-            jax.ShapeDtypeStruct((pairs.shape[0], 1), f32),
+            jax.ShapeDtypeStruct((n, upper, GRAIN, GRAIN), bf16),
+            jax.ShapeDtypeStruct((1, slots), f32),
         ),
-        in_specs=[pl.BlockSpec(memory_space=pl.ANY), vmem, smem, smem, vmem],
-        out_specs=(vmem, vmem),
+        in_specs=[hbm] * 5,
+        out_specs=(hbm, hbm, vmem),
         scratch_shapes=[
+            pltpu.VMEM((n, width), f32),
+            pltpu.SMEM((n,), f32),
+            pltpu.SMEM((n,), jnp.int32),
+            pltpu.VMEM((2, slots), jnp.int32),
             pltpu.VMEM((n, aux, width), bf16),
             pltpu.VMEM((n, aux, width), bf16),
             pltpu.VMEM((width, aux), bf16),
@@ -254,16 +300,27 @@
             pltpu.VMEM((n, width, GRAIN), f32),
             pltpu.VMEM((width, width), f32),
             pltpu.VMEM((n, upper, GRAIN, GRAIN), bf16),
-            pltpu.VMEM((n, upper, GRAIN, GRAIN), bf16),
             pltpu.VMEM((GRAIN, GRAIN), f32),
             pltpu.VMEM((edge, GRAIN), f32),
-            many, many, many, two, two, many, many, two,
+            pltpu.VMEM((n, width, width), f32),
+            pltpu.SemaphoreType.DMA((4,)),
+            many, many, many, two, two, many, many, two, many,
         ],
         compiler_params=pltpu.CompilerParams(
-            collective_id=0, has_side_effects=True, vmem_limit_bytes=52 * 1024 * 1024
+            collective_id=0, has_side_effects=True, vmem_limit_bytes=60 * 1024 * 1024
         ),
-    )(blocks, pao_energy, occ_energy, dom_blocks, pairs)
-    return (energies[:, 0], dens)
+    )(blocks, pao_energy, occ_energy, dom_blocks, pairs.T)
+    each = 2 if n % 2 == 0 else 1
+    square = pl.BlockSpec((each, width, width), lambda k: (k, 0, 0))
+    dens = pl.pallas_call(
+        functools.partial(add_returned, size),
+        grid=(n // each,),
+        out_shape=jax.ShapeDtypeStruct((n, width, width), f32),
+        in_specs=[square, pl.BlockSpec((each, upper, GRAIN, GRAIN), lambda k: (k, 0, 0, 0))],
+        out_specs=square,
+        compiler_params=pltpu.CompilerParams(vmem_limit_bytes=60 * 1024 * 1024),
+    )(part, ret)
+    return (energies.reshape(slots), dens)
 
 
 def solution(mesh):

time: 107 us -> 104 us (0.972)
  local copies, waits for them, and re-layouts: 6.79 us -> 0.52 us
  Pallas kernels: 98 us -> 102 us
    unnamed x8 -> x3, local copies, waits for them, and re-layouts: 6.79 us -> 0.52 us
    pallas_call x0 -> x1, Pallas kernels: none -> 4.96 us  [per_device(): pl.pallas_call(functools.partial(add_returned, size), grid=(n // each,),...]
    pallas_call x1, Pallas kernels: 98 us -> 96.5 us  [per_device(): pl.pallas_call(functools.partial(kernel, size, factor), out_shape=(jax.Sh...]
where the time goes in v3:
time: 104 us; the launch traced here: 103 us
  Pallas kernels  102 us (98%)
    pallas_call x1, Pallas kernels, per_device(): pl.pallas_call(functools.partial(kernel, size, factor), out_shape=(jax.Sh...  96.5 us
    pallas_call x1, Pallas kernels, per_device(): pl.pallas_call(functools.partial(add_returned, size), grid=(n // each,),...  4.96 us

profile of v3, /device:TPU:9, one launch (start us, length us, event | category | flops | bytes accessed | tf_op | source)
XLA Modules:
  0.0 102.7 jit_solution(11717302659511585407)
XLA Ops:
  0.6 96.5 %shard_map.68 = (f32[6,384,384]{2,1,0:T(8,128)}, bf16[6,6,128,128]{3,2,1,0:T(8,128)(2,1)}, f32[1,16]{1,0:T(1,128)}) custom-call(bf16[6,1536,384]{2,1,0:T(8,128)(2,1)} %blocks.1, f32[6,384]{1,0:T(8,128)} %pao_hbm.1, f32[6]{0:T(128)} %occ_hbm.1, s32[6]{0:T(128)} %dom_hbm.1, s32[2,16]{1,0:T(2,128)} %bitcast.2), custom_call_target="tpu_custom_call" | custom-call | tf_op jit(solution)/shard_map/pallas_call | solution.py:278
  97.2 0.0 copy-start
  97.2 5.0 %shard_map.69 = f32[6,384,384]{2,1,0:T(8,128)} custom-call(f32[6,384,384]{2,1,0:T(8,128)} %get-tuple-element.6.part, bf16[6,6,128,128]{3,2,1,0:T(8,128)(2,1)} %get-tuple-element.7.ret), custom_call_target="tpu_custom_call" | custom-call | tf_op jit(solution)/shard_map/pallas_call | solution.py:315
  102.2 0.0 copy-done
  102.2 0.5 copy.8
Async XLA Ops:
  97.2 5.0 %copy-start = (f32[1,16]{1,0:T(1,128)S(1)}, f32[1,16]{1,0:T(1,128)}, u32[]{:S(2)}) copy-start(f32[1,16]{1,0:T(1,128)} %get-tuple-element.5) | copy-start | bytes 196

commit v4 on v3

--- a/solution.py
+++ b/solution.py
@@ -310,7 +310,7 @@
             collective_id=0, has_side_effects=True, vmem_limit_bytes=60 * 1024 * 1024
         ),
     )(blocks, pao_energy, occ_energy, dom_blocks, pairs.T)
-    each = 2 if n % 2 == 0 else 1
+    each = 3 if n % 3 == 0 else 1
     square = pl.BlockSpec((each, width, width), lambda k: (k, 0, 0))
     dens = pl.pallas_call(
         functools.partial(add_returned, size),

time: 104 us -> 103 us (level)
  Pallas kernels: 102 us -> 100 us
    pallas_call x1, Pallas kernels: 4.96 us -> 3.71 us  [per_device(): pl.pallas_call(functools.partial(add_returned, size), grid=(n // each,),...]
where the time goes in v4:
time: 103 us; the launch traced here: 101 us
  Pallas kernels  100 us (97%)
    pallas_call x1, Pallas kernels, per_device(): pl.pallas_call(functools.partial(kernel, size, factor), out_shape=(jax.Sh...  96.5 us
    pallas_call x1, Pallas kernels, per_device(): pl.pallas_call(functools.partial(add_returned, size), grid=(n // each,),...  3.71 us

profile of v4, /device:TPU:9, one launch (start us, length us, event | category | flops | bytes accessed | tf_op | source)
XLA Modules:
  0.0 101.4 jit_solution(1308577292934975487)
XLA Ops:
  0.6 96.5 %shard_map.68 = (f32[6,384,384]{2,1,0:T(8,128)}, bf16[6,6,128,128]{3,2,1,0:T(8,128)(2,1)}, f32[1,16]{1,0:T(1,128)}) custom-call(bf16[6,1536,384]{2,1,0:T(8,128)(2,1)} %blocks.1, f32[6,384]{1,0:T(8,128)} %pao_hbm.1, f32[6]{0:T(128)} %occ_hbm.1, s32[6]{0:T(128)} %dom_hbm.1, s32[2,16]{1,0:T(2,128)} %bitcast.2), custom_call_target="tpu_custom_call" | custom-call | tf_op jit(solution)/shard_map/pallas_call | solution.py:278
  97.2 0.0 copy-start
  97.2 3.7 %shard_map.69 = f32[6,384,384]{2,1,0:T(8,128)} custom-call(f32[6,384,384]{2,1,0:T(8,128)} %get-tuple-element.6.part, bf16[6,6,128,128]{3,2,1,0:T(8,128)(2,1)} %get-tuple-element.7.ret), custom_call_target="tpu_custom_call" | custom-call | tf_op jit(solution)/shard_map/pallas_call | solution.py:315
  100.9 0.0 copy-done
  100.9 0.5 copy.8
Async XLA Ops:
  97.2 3.7 %copy-start = (f32[1,16]{1,0:T(1,128)S(1)}, f32[1,16]{1,0:T(1,128)}, u32[]{:S(2)}) copy-start(f32[1,16]{1,0:T(1,128)} %get-tuple-element.5) | copy-start | bytes 196
